TPU v7x, 32 devices: a whole 2x2x4 slice. The times are simulated.
32 devices in a mesh: row: 8 (over z, x), col: 4 (over y, core).
Axes of the slice: x: 2, y: 2, z: 4, core: 2. Of those that a mesh axis runs over, the one named last changes fastest.
Arguments:
- matrix: float32 [3584, 3584], P('row', 'col'), may hold values from -3 to 3
- reflectors: float32 [1, 64, 3584], P(None, None, 'row'), may hold values from -0.1875 to 0.1875
- factors: float32 [1, 64, 64], replicated, may hold values from -0.1 to 2, as said below
Outputs:
- updated: float32 [3584, 3584], P('row', 'col')
- companions: float32 [1, 64, 3584], P(None, None, 'row')
Inputs may be any that keep to these rules, and one draw needn't show every extreme that they name: `factors`: each factor is upper triangular (zero below the diagonal) with diagonal entries between 1 and 2.
All inputs are finite; a program needn't handle non-finite values.
Results may differ from a plain program's by a relative error of at most 0.0001.
Values sent between devices are 32-bit elements; how exact they have to be, the bound alone decides.
A program may use at most 64 MiB of HBM per device.

v0:
```python
import functools

import jax
import jax.numpy as jnp
from jax import lax
from jax.experimental import pallas as pl
from jax.experimental.pallas import tpu as pltpu
from jax.sharding import PartitionSpec as P

MESH = pl.DeviceIdType.MESH


def split(x):
    hi = x.astype(jnp.bfloat16)
    return hi, (x - hi.astype(jnp.float32)).astype(jnp.bfloat16)


def dot(a, b, da, db):
    return lax.dot_general(a, b, (((da,), (db,)), ((), ())), preferred_element_type=jnp.float32)


def dot3(a, b, da, db):
    ah, al = split(a)
    bh, bl = split(b)
    return dot(ah, bh, da, db) + (dot(ah, bl, da, db) + dot(al, bh, da, db))


def kernel(
    nr, nc, v_hbm, a_hbm, f_hbm, out_ref, w_ref,
    a_ref, a_hi, a_lo, v_ref, f_ref, vrecv, pbuf, precv, yown, yrecv, yrow, srow, spart, sown, sfull,
    in_sem, gv_send, gv_recv, rs_send, rs_recv, gy_send, gy_recv, yr_send, yr_recv, sr_send, sr_recv, sc_send, sc_recv,
):
    ratio, half = nr // nc, nc // 2
    r, c = lax.axis_index("row"), lax.axis_index("col")
    g, i = r // ratio, r % ratio
    line, core = c // 2, c % 2
    aligned = g % 2 == core
    n = v_ref.shape[2]
    b = f_ref.shape[0]
    h = b // nc

    v_copy = pltpu.make_async_copy(v_hbm, v_ref, in_sem.at[0])
    a_copy = pltpu.make_async_copy(a_hbm, a_ref, in_sem.at[1])
    f_copy = pltpu.make_async_copy(f_hbm, f_ref, in_sem.at[2])
    v_copy.start()
    f_copy.start()
    a_copy.start()

    def remote(src, dst, send, recv, row, col):
        return pltpu.make_async_remote_copy(
            src_ref=src, dst_ref=dst, send_sem=send, recv_sem=recv, device_id=(row, col), device_id_type=MESH
        )

    row_peers = [lax.rem(r + k, nr) for k in range(1, nr)]
    col_peers = [lax.rem(c + k, nc) for k in range(1, nc)]

    def signal(row, col):
        pl.semaphore_signal(barrier, inc=1, device_id=(row, col), device_id_type=MESH)

    barrier = pltpu.get_barrier_semaphore()
    for t in row_peers:
        signal(t, c)
    for q in col_peers:
        signal(r, q)
    for d in range(ratio):
        for e in range(half):
            if d or e:
                signal(g * ratio + lax.rem(i + d, ratio), lax.rem(line + e, half) * 2 + core)
    for j in range(half):
        for e in range(2):
            row = (lax.rem(g // 2 + j, half) * 2 + core) * ratio + i
            col = line * 2 + lax.rem(core + e, 2)
            if j or e:
                signal(row, col)
            else:
                pl.when(jnp.logical_not(aligned))(functools.partial(signal, row, col))
    count = nr - 1 + nc - 1 + ratio * half - 1 + nc
    pl.semaphore_wait(barrier, count - jnp.where(aligned, 1, 0))

    relay = ratio * nc

    class Gather:
        def __init__(self, src, buf, send, recv):
            self.src, self.buf, self.send, self.recv = src, buf, send, recv
            slot = jnp.where(g // 2 == line, i * nc + c, relay + (g // 2) * 2 + core)
            self.first = [
                remote(
                    src, buf.at[slot], send.at[j], recv.at[slot],
                    lax.rem(g + j, nc) * ratio + i, line * 2 + g % 2,
                )
                for j in range(nc)
            ]
            for copy in self.first[1:]:
                copy.start()
            pl.when(jnp.logical_not(aligned))(self.first[0].start)

            @pl.when(aligned)
            def _():
                buf[slot] = src[...]

        def forward(self):
            self.second = []
            k = nc
            for j in list(range(1, half)) + [0]:
                a = lax.rem(line + j, half)
                for e in range(2):
                    final = i * nc + line * 2 + e
                    slot = relay + a * 2 + e if j else final
                    mine = jnp.logical_and(a * 2 + core == g, e == core)
                    arrival = remote(self.src, self.buf.at[slot], self.send.at[0], self.recv.at[slot], r, c)
                    pl.when(jnp.logical_not(mine))(arrival.wait_recv)
                    for d in range(0 if j else 1, ratio):
                        copy = remote(
                            self.buf.at[slot], self.buf.at[final], self.send.at[k], self.recv.at[final],
                            g * ratio + lax.rem(i + d, ratio), a * 2 + core,
                        )
                        copy.start()
                        self.second.append(copy)
                        k += 1

        def wait(self):
            for d in range(ratio):
                for e in range(half):
                    for k in range(2):
                        if d or e:
                            slot = lax.rem(i + d, ratio) * nc + lax.rem(line + e, half) * 2 + k
                            remote(
                                self.src, self.buf.at[slot], self.send.at[0], self.recv.at[slot], r, c
                            ).wait_recv()

        def columns(self):
            return jnp.concatenate(
                [
                    jnp.concatenate([self.buf[t * nc + q] for q in range(nc)], axis=0)
                    for t in range(ratio)
                ],
                axis=1,
            )

        def end(self):
            pl.when(jnp.logical_not(aligned))(self.first[0].wait_send)
            for copy in self.first[1:] + self.second:
                copy.wait_send()

    v_copy.wait()
    gv = Gather(v_ref.at[c], vrecv, gv_send, gv_recv)
    gv.forward()

    f_copy.wait()
    a_copy.wait()
    hi, lo = split(a_ref[...])
    a_hi[...] = hi
    a_lo[...] = lo
    v_rows = jnp.concatenate([v_ref[q] for q in range(nc)], axis=0)

    gv.wait()
    v_cols = gv.columns()
    vh, vl = split(v_cols)
    both = dot(jnp.concatenate([vh, vl], axis=0), a_hi[...], 1, 1)
    partial = both[:b] + (both[b:] + dot(vh, a_lo[...], 1, 1))
    term = dot3(v_rows, partial, 1, 1)
    for q in range(nc):
        pbuf[q, :, :n] = partial[q * h:(q + 1) * h]
        pbuf[q, :, n:] = term[q * h:(q + 1) * h]

    rs = [remote(pbuf.at[q], precv.at[c], rs_send.at[k], rs_recv.at[c], r, q) for k, q in enumerate(col_peers)]
    for copy in rs:
        copy.start()
    total = pbuf[c]
    for k, q in enumerate(col_peers):
        remote(pbuf.at[q], precv.at[q], rs_send.at[k], rs_recv.at[q], r, q).wait_recv()
        total = total + precv[q]
    yown[...] = total[:, :n]
    spart[...] = total[:, n:]
    srow[r] = total[:, n:]

    gy = Gather(yown, yrecv, gy_send, gy_recv)
    sr = [remote(spart, srow.at[r], sr_send.at[k], sr_recv.at[r], t, c) for k, t in enumerate(row_peers)]
    for copy in sr:
        copy.start()
    yr = [remote(yown, yrow.at[c], yr_send.at[k], yr_recv.at[c], r, q) for k, q in enumerate(col_peers)]
    for copy in yr:
        copy.start()
    yrow[c] = yown[...]
    gy.forward()

    for k, t in enumerate(row_peers):
        remote(spart, srow.at[t], sr_send.at[k], sr_recv.at[t], t, c).wait_recv()
    s = srow[0]
    for t in range(1, nr):
        s = s + srow[t]
    sown[...] = s
    sfull[c] = s
    sc = [remote(sown, sfull.at[c], sc_send.at[k], sc_recv.at[c], r, q) for k, q in enumerate(col_peers)]
    for copy in sc:
        copy.start()
    for k, q in enumerate(col_peers):
        remote(sown, sfull.at[q], sc_send.at[k], sc_recv.at[q], r, q).wait_recv()
    square = jnp.concatenate([sfull[q] for q in range(nc)], axis=0)
    factor = f_ref[...]
    mixing = 0.5 * dot3(dot3(square, factor, 1, 0), factor, 0, 0)

    for k, q in enumerate(col_peers):
        remote(yown, yrow.at[q], yr_send.at[k], yr_recv.at[q], r, q).wait_recv()
    y_rows = jnp.concatenate([yrow[q] for q in range(nc)], axis=0)
    w_rows = dot3(factor, y_rows, 0, 0) - dot3(mixing, v_rows, 1, 0)
    w_ref[0] = w_rows

    gy.wait()
    w_cols = dot3(factor, gy.columns(), 0, 0) - dot3(mixing, v_cols, 1, 0)

    lh, ll = split(jnp.concatenate([v_rows, w_rows], axis=0))
    rh, rl = split(jnp.concatenate([w_cols, v_cols], axis=0))
    left = jnp.concatenate([lh, lh, ll], axis=0)
    right = jnp.concatenate([rh, rl, rh], axis=0)
    out_ref[...] = a_ref[...] - dot(left, right, 0, 0)

    gv.end()
    gy.end()
    for copy in rs + sr + yr + sc:
        copy.wait_send()


def shards(matrix, reflectors, factors):
    nr, nc = lax.axis_size("row"), lax.axis_size("col")
    _, b, n = reflectors.shape
    m, k = matrix.shape
    ratio, h = nr // nc, b // nc
    f32 = jnp.float32
    dma = pltpu.SemaphoreType.DMA
    vmem = pl.BlockSpec(memory_space=pltpu.VMEM)
    hbm = pl.BlockSpec(memory_space=pltpu.HBM)
    slots = ratio * nc + nc
    sends = nc + 2 * (ratio * (nc // 2) - 1)
    return pl.pallas_call(
        functools.partial(kernel, nr, nc),
        out_shape=(jax.ShapeDtypeStruct((m, k), f32), jax.ShapeDtypeStruct((1, b, n), f32)),
        in_specs=[hbm, hbm, hbm],
        out_specs=(vmem, vmem),
        scratch_shapes=[
            pltpu.VMEM((m, k), f32),
            pltpu.VMEM((m, k), jnp.bfloat16),
            pltpu.VMEM((m, k), jnp.bfloat16),
            pltpu.VMEM((nc, h, n), f32),
            pltpu.VMEM((b, b), f32),
            pltpu.VMEM((slots, h, n), f32),
            pltpu.VMEM((nc, h, n + b), f32),
            pltpu.VMEM((nc, h, n + b), f32),
            pltpu.VMEM((h, n), f32),
            pltpu.VMEM((slots, h, n), f32),
            pltpu.VMEM((nc, h, n), f32),
            pltpu.VMEM((nr, h, b), f32),
            pltpu.VMEM((h, b), f32),
            pltpu.VMEM((h, b), f32),
            pltpu.VMEM((nc, h, b), f32),
            dma((3,)),
            dma((sends,)), dma((slots,)),
            dma((nc - 1,)), dma((nc,)),
            dma((sends,)), dma((slots,)),
            dma((nc - 1,)), dma((nc,)),
            dma((nr - 1,)), dma((nr,)),
            dma((nc - 1,)), dma((nc,)),
        ],
        compiler_params=pltpu.CompilerParams(
            collective_id=0, has_side_effects=True, vmem_limit_bytes=48 * 1024 * 1024
        ),
        name="reflector_update",
    )(*(pltpu.with_memory_space_constraint(x, pltpu.HBM) for x in (reflectors.reshape(nc, h, n), matrix, factors[0])))


def solution(mesh):
    return jax.shard_map(
        shards,
        mesh=mesh,
        in_specs=(P("row", "col"), P(None, None, "row"), P()),
        out_specs=(P("row", "col"), P(None, None, "row")),
        check_vma=False,
    )
```

profile of v0, /device:TPU:0, one launch (start us, length us, event | category | flops | bytes accessed | tf_op | source)
XLA Modules:
  0.0 33.3 jit_solution(18080306662124323730)
XLA Ops:
  0.6 30.9 %reflector_update.1 = (f32[448,896]{1,0:T(8,128)S(1)}, f32[1,64,448]{2,1,0:T(8,128)S(1)}) custom-call(f32[4,16,448]{2,1,0:T(8,128)} %bitcast.2, f32[448,896]{1,0:T(8,128)} %a_hbm.1, f32[64,64]{1,0:T(8,128)} %bitcast.3), custom_call_target="tpu_custom_call" | custom-call | tf_op jit(solution)/shard_map/reflector_update/pallas_call | solution.py:235
  31.5 1.2 %copy.7 = f32[448,896]{1,0:T(8,128)} copy(f32[448,896]{1,0:T(8,128)S(1)} %get-tuple-element.4) | data formatting | bytes 3211264
  32.7 0.7 %copy.8 = f32[1,64,448]{2,1,0:T(8,128)} copy(f32[1,64,448]{2,1,0:T(8,128)S(1)} %get-tuple-element.5) | data formatting | bytes 229376
where the time goes:
time: 33.5 us; the launch traced here: 33.3 us
  Pallas kernels  30.9 us (92%)
  local copies, waits for them, and re-layouts  1.81 us (5%)
  between operations  0.64 us (2%)
    pallas_call x1, Pallas kernels, shards(): pl.pallas_call(functools.partial(kernel, nr, nc), out_shape=(jax.ShapeDty...  30.9 us
    unnamed x2, local copies, waits for them, and re-layouts  1.81 us

commit v1 on v0

--- a/solution.py
+++ b/solution.py
@@ -26,8 +26,8 @@
 
 
 def kernel(
-    nr, nc, v_hbm, a_hbm, f_hbm, out_ref, w_ref,
-    a_ref, a_hi, a_lo, v_ref, f_ref, vrecv, pbuf, precv, yown, yrecv, yrow, srow, spart, sown, sfull,
+    nr, nc, v_hbm, a_hbm, f_hbm, a_ref, left_ref, right_ref, w_ref,
+    a_hi, a_lo, v_ref, f_ref, vrecv, pbuf, precv, yown, yrecv, yrow, srow, spart, sown, sfull,
     in_sem, gv_send, gv_recv, rs_send, rs_recv, gy_send, gy_recv, yr_send, yr_recv, sr_send, sr_recv, sc_send, sc_recv,
 ):
     ratio, half = nr // nc, nc // 2
@@ -82,7 +82,7 @@
     class Gather:
         def __init__(self, src, buf, send, recv):
             self.src, self.buf, self.send, self.recv = src, buf, send, recv
-            slot = jnp.where(g // 2 == line, i * nc + c, relay + (g // 2) * 2 + core)
+            self.slot = slot = jnp.where(g // 2 == line, i * nc + c, relay + (g // 2) * 2 + core)
             self.first = [
                 remote(
                     src, buf.at[slot], send.at[j], recv.at[slot],
@@ -94,11 +94,11 @@
                 copy.start()
             pl.when(jnp.logical_not(aligned))(self.first[0].start)
 
+        def forward(self, own):
             @pl.when(aligned)
             def _():
-                buf[slot] = src[...]
-
-        def forward(self):
+                self.buf[self.slot] = own[...]
+
             self.second = []
             k = nc
             for j in list(range(1, half)) + [0]:
@@ -142,9 +142,9 @@
             for copy in self.first[1:] + self.second:
                 copy.wait_send()
 
+    gv = Gather(v_hbm.at[c], vrecv, gv_send, gv_recv)
     v_copy.wait()
-    gv = Gather(v_ref.at[c], vrecv, gv_send, gv_recv)
-    gv.forward()
+    gv.forward(v_ref.at[c])
 
     f_copy.wait()
     a_copy.wait()
@@ -174,15 +174,14 @@
     spart[...] = total[:, n:]
     srow[r] = total[:, n:]
 
-    gy = Gather(yown, yrecv, gy_send, gy_recv)
     sr = [remote(spart, srow.at[r], sr_send.at[k], sr_recv.at[r], t, c) for k, t in enumerate(row_peers)]
     for copy in sr:
         copy.start()
+    gy = Gather(yown, yrecv, gy_send, gy_recv)
     yr = [remote(yown, yrow.at[c], yr_send.at[k], yr_recv.at[c], r, q) for k, q in enumerate(col_peers)]
     for copy in yr:
         copy.start()
     yrow[c] = yown[...]
-    gy.forward()
 
     for k, t in enumerate(row_peers):
         remote(spart, srow.at[t], sr_send.at[k], sr_recv.at[t], t, c).wait_recv()
@@ -194,31 +193,46 @@
     sc = [remote(sown, sfull.at[c], sc_send.at[k], sc_recv.at[c], r, q) for k, q in enumerate(col_peers)]
     for copy in sc:
         copy.start()
+    gy.forward(yown)
+
+    factor = f_ref[...]
+    for k, q in enumerate(col_peers):
+        remote(yown, yrow.at[q], yr_send.at[k], yr_recv.at[q], r, q).wait_recv()
+    y_rows = jnp.concatenate([yrow[q] for q in range(nc)], axis=0)
+    x_rows = dot3(factor, y_rows, 0, 0)
     for k, q in enumerate(col_peers):
         remote(sown, sfull.at[q], sc_send.at[k], sc_recv.at[q], r, q).wait_recv()
     square = jnp.concatenate([sfull[q] for q in range(nc)], axis=0)
-    factor = f_ref[...]
     mixing = 0.5 * dot3(dot3(square, factor, 1, 0), factor, 0, 0)
-
-    for k, q in enumerate(col_peers):
-        remote(yown, yrow.at[q], yr_send.at[k], yr_recv.at[q], r, q).wait_recv()
-    y_rows = jnp.concatenate([yrow[q] for q in range(nc)], axis=0)
-    w_rows = dot3(factor, y_rows, 0, 0) - dot3(mixing, v_rows, 1, 0)
+    w_rows = x_rows - dot3(mixing, v_rows, 1, 0)
     w_ref[0] = w_rows
+    lh, ll = split(jnp.concatenate([v_rows, w_rows], axis=0).T)
+    left_ref[...] = jnp.concatenate([lh, lh, ll], axis=1)
+    right_ref[b:2 * b] = vh
+    right_ref[3 * b:4 * b] = vl
+    right_ref[5 * b:] = vh
+    mixed = dot3(mixing, v_cols, 1, 0)
 
     gy.wait()
-    w_cols = dot3(factor, gy.columns(), 0, 0) - dot3(mixing, v_cols, 1, 0)
-
-    lh, ll = split(jnp.concatenate([v_rows, w_rows], axis=0))
-    rh, rl = split(jnp.concatenate([w_cols, v_cols], axis=0))
-    left = jnp.concatenate([lh, lh, ll], axis=0)
-    right = jnp.concatenate([rh, rl, rh], axis=0)
-    out_ref[...] = a_ref[...] - dot(left, right, 0, 0)
+    wh, wl = split(dot3(factor, gy.columns(), 0, 0) - mixed)
+    right_ref[:b] = wh
+    right_ref[2 * b:3 * b] = wl
+    right_ref[4 * b:5 * b] = wh
 
     gv.end()
     gy.end()
     for copy in rs + sr + yr + sc:
         copy.wait_send()
+
+
+def update(a_ref, left_ref, right_ref, w_ref, out_ref, companion_ref):
+    size = out_ref.shape[0]
+    rows = pl.ds(pl.multiple_of(pl.program_id(0) * size, size), size)
+    out_ref[...] = a_ref[rows, :] - dot(left_ref[rows, :], right_ref[...], 1, 0)
+
+    @pl.when(pl.program_id(0) == 0)
+    def _():
+        companion_ref[...] = w_ref[...]
 
 
 def shards(matrix, reflectors, factors):
@@ -232,13 +246,17 @@
     hbm = pl.BlockSpec(memory_space=pltpu.HBM)
     slots = ratio * nc + nc
     sends = nc + 2 * (ratio * (nc // 2) - 1)
-    return pl.pallas_call(
+    held = pl.pallas_call(
         functools.partial(kernel, nr, nc),
-        out_shape=(jax.ShapeDtypeStruct((m, k), f32), jax.ShapeDtypeStruct((1, b, n), f32)),
+        out_shape=(
+            jax.ShapeDtypeStruct((m, k), f32),
+            jax.ShapeDtypeStruct((m, 6 * b), jnp.bfloat16),
+            jax.ShapeDtypeStruct((6 * b, k), jnp.bfloat16),
+            jax.ShapeDtypeStruct((1, b, n), f32),
+        ),
         in_specs=[hbm, hbm, hbm],
-        out_specs=(vmem, vmem),
+        out_specs=(vmem,) * 4,
         scratch_shapes=[
-            pltpu.VMEM((m, k), f32),
             pltpu.VMEM((m, k), jnp.bfloat16),
             pltpu.VMEM((m, k), jnp.bfloat16),
             pltpu.VMEM((nc, h, n), f32),
@@ -262,10 +280,23 @@
             dma((nc - 1,)), dma((nc,)),
         ],
         compiler_params=pltpu.CompilerParams(
-            collective_id=0, has_side_effects=True, vmem_limit_bytes=48 * 1024 * 1024
+            collective_id=0, has_side_effects=True, vmem_limit_bytes=32 * 1024 * 1024
         ),
         name="reflector_update",
     )(*(pltpu.with_memory_space_constraint(x, pltpu.HBM) for x in (reflectors.reshape(nc, h, n), matrix, factors[0])))
+    steps = 4
+    return pl.pallas_call(
+        update,
+        grid=(steps,),
+        out_shape=(jax.ShapeDtypeStruct((m, k), f32), jax.ShapeDtypeStruct((1, b, n), f32)),
+        in_specs=[vmem] * 4,
+        out_specs=(
+            pl.BlockSpec((m // steps, k), lambda t: (t, 0)),
+            pl.BlockSpec((1, b, n), lambda t: (0, 0, 0)),
+        ),
+        compiler_params=pltpu.CompilerParams(vmem_limit_bytes=16 * 1024 * 1024),
+        name="tile_update",
+    )(*held)
 
 
 def solution(mesh):

time: 33.5 us -> 33.2 us (level)
  local copies, waits for them, and re-layouts: 1.81 us -> 0 us
  Pallas kernels: 30.9 us -> 32.4 us
    pallas_call x0 -> x1, Pallas kernels: none -> 2.46 us  [shards(): pl.pallas_call(update, grid=(steps,), out_shape=(jax.ShapeDtypeStruct((m,...]
    unnamed x2 -> x0, local copies, waits for them, and re-layouts: 1.81 us -> none
    pallas_call x1, Pallas kernels: 30.9 us -> 30 us  [shards(): pl.pallas_call(functools.partial(kernel, nr, nc), out_shape=(jax.ShapeDty...]
where the time goes in v1:
time: 33.2 us; the launch traced here: 33.1 us
  Pallas kernels  32.4 us (98%)
  between operations  0.64 us (2%)
    pallas_call x1, Pallas kernels, shards(): pl.pallas_call(functools.partial(kernel, nr, nc), out_shape=(jax.ShapeDty...  30 us
    pallas_call x1, Pallas kernels, shards(): pl.pallas_call(update, grid=(steps,), out_shape=(jax.ShapeDtypeStruct((m,...  2.46 us

profile of v1, /device:TPU:0, one launch (start us, length us, event | category | flops | bytes accessed | tf_op | source)
XLA Modules:
  0.0 33.1 jit_solution(10390520794390393299)
XLA Ops:
  0.6 30.0 %reflector_update.1 = (f32[448,896]{1,0:T(8,128)S(1)}, bf16[448,384]{1,0:T(8,128)(2,1)S(1)}, bf16[384,896]{1,0:T(8,128)(2,1)S(1)}, f32[1,64,448]{2,1,0:T(8,128)S(1)}) custom-call(f32[4,16,448]{2,1,0:T(8,128)} %bitcast.2, f32[448,896]{1,0:T(8,128)} %a_hbm.1, f32[64,64]{1,0:T(8,128)} %bitcast.3), custom_call_target="tpu_custom_call" | custom-call | tf_op jit(solution)/shard_map/reflector_update/pallas_call | solution.py:249
  30.6 2.5 %tile_update.1 = (f32[448,896]{1,0:T(8,128)}, f32[1,64,448]{2,1,0:T(8,128)}) custom-call(f32[448,896]{1,0:T(8,128)S(1)} %get-tuple-element.6.a_ref, bf16[448,384]{1,0:T(8,128)(2,1)S(1)} %get-tuple-element.7.left_ref, bf16[384,896]{1,0:T(8,128)(2,1)S(1)} %get-tuple-element.8.right_ref, f32[1,64,448]{2,1,0:T(8,128)S(1)} %get-tuple-element.9.w_ref), custom_call_target="tpu_custom_call" | custom-call | tf_op jit(solution)/shard_map/tile_update/pallas_call | solution.py:288

commit v2 on v1

--- a/solution.py
+++ b/solution.py
@@ -27,17 +27,18 @@
 
 def kernel(
     nr, nc, v_hbm, a_hbm, f_hbm, a_ref, left_ref, right_ref, w_ref,
-    a_hi, a_lo, v_ref, f_ref, vrecv, pbuf, precv, yown, yrecv, yrow, srow, spart, sown, sfull,
-    in_sem, gv_send, gv_recv, rs_send, rs_recv, gy_send, gy_recv, yr_send, yr_recv, sr_send, sr_recv, sc_send, sc_recv,
+    v_ref, f_ref, vown, vrecv, zbuf, zrecv, ycols, yhalf, yrow, spart, scol, sfull,
+    in_sem, gv_send, gv_recv, rs_send, rs_recv, ag_send, ag_recv, yr_send, yr_recv, sc_send, sc_recv, sr_send, sr_recv,
 ):
     ratio, half = nr // nc, nc // 2
     r, c = lax.axis_index("row"), lax.axis_index("col")
     g, i = r // ratio, r % ratio
     line, core = c // 2, c % 2
     aligned = g % 2 == core
-    n = v_ref.shape[2]
+    home = r // ratio
+    n = v_hbm.shape[2]
     b = f_ref.shape[0]
-    h = b // nc
+    hr = b // nr
 
     v_copy = pltpu.make_async_copy(v_hbm, v_ref, in_sem.at[0])
     a_copy = pltpu.make_async_copy(a_hbm, a_ref, in_sem.at[1])
@@ -62,20 +63,19 @@
         signal(t, c)
     for q in col_peers:
         signal(r, q)
-    for d in range(ratio):
-        for e in range(half):
-            if d or e:
-                signal(g * ratio + lax.rem(i + d, ratio), lax.rem(line + e, half) * 2 + core)
-    for j in range(half):
-        for e in range(2):
-            row = (lax.rem(g // 2 + j, half) * 2 + core) * ratio + i
-            col = line * 2 + lax.rem(core + e, 2)
-            if j or e:
-                signal(row, col)
-            else:
-                pl.when(jnp.logical_not(aligned))(functools.partial(signal, row, col))
-    count = nr - 1 + nc - 1 + ratio * half - 1 + nc
-    pl.semaphore_wait(barrier, count - jnp.where(aligned, 1, 0))
+    for d in range(1, ratio):
+        for e in range(1, half):
+            signal(g * ratio + lax.rem(i + d, ratio), lax.rem(line + e, half) * 2 + core)
+    for a in range(half):
+        signal((a * 2 + core) * ratio + i, line * 2 + 1 - core)
+
+    @pl.when(home != c)
+    def _():
+        for t in range(nr):
+            signal(t, home)
+
+    count = nr - 1 + nc - 1 + (ratio - 1) * (half - 1) + ratio * (nc - 1)
+    pl.semaphore_wait(barrier, count + jnp.where(aligned, 0, nc))
 
     relay = ratio * nc
 
@@ -131,7 +131,7 @@
         def columns(self):
             return jnp.concatenate(
                 [
-                    jnp.concatenate([self.buf[t * nc + q] for q in range(nc)], axis=0)
+                    jnp.concatenate([self.buf[t * nc + q, :, :n] for q in range(nc)], axis=0)
                     for t in range(ratio)
                 ],
                 axis=1,
@@ -142,87 +142,114 @@
             for copy in self.first[1:] + self.second:
                 copy.wait_send()
 
-    gv = Gather(v_hbm.at[c], vrecv, gv_send, gv_recv)
     v_copy.wait()
-    gv.forward(v_ref.at[c])
-
+    vown[:, :n] = v_ref[c]
+    gv = Gather(vown, vrecv, gv_send, gv_recv)
+    v_rows = jnp.concatenate([v_ref[q] for q in range(nc)], axis=0)
+    vh, vl = split(v_rows)
     f_copy.wait()
     a_copy.wait()
-    hi, lo = split(a_ref[...])
-    a_hi[...] = hi
-    a_lo[...] = lo
-    v_rows = jnp.concatenate([v_ref[q] for q in range(nc)], axis=0)
-
+    ah, al = split(a_ref[...])
+    both = dot(jnp.concatenate([vh, vl], axis=0), ah, 1, 0)
+    z = both[:b] + (both[b:] + dot(vh, al, 1, 0))
+    for t in range(nr):
+        zbuf[t] = z[t * hr:(t + 1) * hr]
+
+    rs = [remote(zbuf.at[t], zrecv.at[r], rs_send.at[k], rs_recv.at[r], t, c) for k, t in enumerate(row_peers)]
+    for copy in rs:
+        copy.start()
+    zrecv[r] = zbuf[r]
+
+    gv.forward(vown)
+    left_ref[:, :b] = vh.T
+    left_ref[:, 2 * b:3 * b] = vh.T
+    left_ref[:, 4 * b:5 * b] = vl.T
     gv.wait()
     v_cols = gv.columns()
-    vh, vl = split(v_cols)
-    both = dot(jnp.concatenate([vh, vl], axis=0), a_hi[...], 1, 1)
-    partial = both[:b] + (both[b:] + dot(vh, a_lo[...], 1, 1))
-    term = dot3(v_rows, partial, 1, 1)
-    for q in range(nc):
-        pbuf[q, :, :n] = partial[q * h:(q + 1) * h]
-        pbuf[q, :, n:] = term[q * h:(q + 1) * h]
-
-    rs = [remote(pbuf.at[q], precv.at[c], rs_send.at[k], rs_recv.at[c], r, q) for k, q in enumerate(col_peers)]
-    for copy in rs:
+    ch, cl = split(v_cols)
+    right_ref[b:2 * b] = ch
+    right_ref[3 * b:4 * b] = cl
+    right_ref[5 * b:] = ch
+
+    for k, t in enumerate(row_peers):
+        remote(zbuf.at[t], zrecv.at[t], rs_send.at[k], rs_recv.at[t], t, c).wait_recv()
+    y = zrecv[0]
+    for t in range(1, nr):
+        y = y + zrecv[t]
+    ycols[r] = y
+    for e in range(ratio):
+        yhalf[e, :, :n] = y[:, e * n:(e + 1) * n]
+    ag = [remote(ycols.at[r], ycols.at[r], ag_send.at[k], ag_recv.at[r], t, c) for k, t in enumerate(row_peers)]
+    for copy in ag:
         copy.start()
-    total = pbuf[c]
+
+    scol[c, :, :b] = dot3(y, v_cols, 1, 1)
+    sc = [remote(scol.at[c], scol.at[c], sc_send.at[k], sc_recv.at[c], r, q) for k, q in enumerate(col_peers)]
+    for copy in sc:
+        copy.start()
+
+    yr = []
+    for d in range(nc):
+        q = lax.rem(c + d, nc)
+        for e in range(ratio):
+            t = c * ratio + e
+            copy = remote(yhalf.at[e], yrow.at[r], yr_send.at[d, e], yr_recv.at[r], t, q)
+            yr.append((d or None, t, copy))
+            if d:
+                copy.start()
+            else:
+                pl.when(t != r)(copy.start)
+
+    @pl.when(home == c)
+    def _():
+        yrow[r] = yhalf[i]
+
     for k, q in enumerate(col_peers):
-        remote(pbuf.at[q], precv.at[q], rs_send.at[k], rs_recv.at[q], r, q).wait_recv()
-        total = total + precv[q]
-    yown[...] = total[:, :n]
-    spart[...] = total[:, n:]
-    srow[r] = total[:, n:]
-
-    sr = [remote(spart, srow.at[r], sr_send.at[k], sr_recv.at[r], t, c) for k, t in enumerate(row_peers)]
+        remote(scol.at[c], scol.at[q], sc_send.at[k], sc_recv.at[q], r, q).wait_recv()
+    s = scol[0]
+    for q in range(1, nc):
+        s = s + scol[q]
+    spart[...] = s
+    sfull[r] = s
+    sr = [remote(spart, sfull.at[r], sr_send.at[k], sr_recv.at[r], t, c) for k, t in enumerate(row_peers)]
     for copy in sr:
         copy.start()
-    gy = Gather(yown, yrecv, gy_send, gy_recv)
-    yr = [remote(yown, yrow.at[c], yr_send.at[k], yr_recv.at[c], r, q) for k, q in enumerate(col_peers)]
-    for copy in yr:
-        copy.start()
-    yrow[c] = yown[...]
-
+
+    factor = f_ref[...]
+    for d in range(nr):
+        t = lax.rem(r + d, nr)
+        arrival = remote(yhalf.at[0], yrow.at[t], yr_send.at[0, 0], yr_recv.at[t], t, home)
+        if d:
+            arrival.wait_recv()
+        else:
+            pl.when(home != c)(arrival.wait_recv)
+    x_rows = dot3(factor, jnp.concatenate([yrow[t, :, :n] for t in range(nr)], axis=0), 0, 0)
     for k, t in enumerate(row_peers):
-        remote(spart, srow.at[t], sr_send.at[k], sr_recv.at[t], t, c).wait_recv()
-    s = srow[0]
-    for t in range(1, nr):
-        s = s + srow[t]
-    sown[...] = s
-    sfull[c] = s
-    sc = [remote(sown, sfull.at[c], sc_send.at[k], sc_recv.at[c], r, q) for k, q in enumerate(col_peers)]
-    for copy in sc:
-        copy.start()
-    gy.forward(yown)
-
-    factor = f_ref[...]
-    for k, q in enumerate(col_peers):
-        remote(yown, yrow.at[q], yr_send.at[k], yr_recv.at[q], r, q).wait_recv()
-    y_rows = jnp.concatenate([yrow[q] for q in range(nc)], axis=0)
-    x_rows = dot3(factor, y_rows, 0, 0)
-    for k, q in enumerate(col_peers):
-        remote(sown, sfull.at[q], sc_send.at[k], sc_recv.at[q], r, q).wait_recv()
-    square = jnp.concatenate([sfull[q] for q in range(nc)], axis=0)
-    mixing = 0.5 * dot3(dot3(square, factor, 1, 0), factor, 0, 0)
+        remote(ycols.at[r], ycols.at[t], ag_send.at[k], ag_recv.at[t], t, c).wait_recv()
+    x_cols = dot3(factor, jnp.concatenate([ycols[t] for t in range(nr)], axis=0), 0, 0)
+    for k, t in enumerate(row_peers):
+        remote(spart, sfull.at[t], sr_send.at[k], sr_recv.at[t], t, c).wait_recv()
+    square = jnp.concatenate([sfull[t, :, :b] for t in range(nr)], axis=0)
+    mixing = 0.5 * dot3(factor, dot3(square, factor, 1, 0), 0, 0)
     w_rows = x_rows - dot3(mixing, v_rows, 1, 0)
     w_ref[0] = w_rows
-    lh, ll = split(jnp.concatenate([v_rows, w_rows], axis=0).T)
-    left_ref[...] = jnp.concatenate([lh, lh, ll], axis=1)
-    right_ref[b:2 * b] = vh
-    right_ref[3 * b:4 * b] = vl
-    right_ref[5 * b:] = vh
-    mixed = dot3(mixing, v_cols, 1, 0)
-
-    gy.wait()
-    wh, wl = split(dot3(factor, gy.columns(), 0, 0) - mixed)
+    lh, ll = split(w_rows.T)
+    left_ref[:, b:2 * b] = lh
+    left_ref[:, 3 * b:4 * b] = lh
+    left_ref[:, 5 * b:] = ll
+    wh, wl = split(x_cols - dot3(mixing, v_cols, 1, 0))
     right_ref[:b] = wh
     right_ref[2 * b:3 * b] = wl
     right_ref[4 * b:5 * b] = wh
 
     gv.end()
-    gy.end()
-    for copy in rs + sr + yr + sc:
+    for copy in rs + ag + sc + sr:
         copy.wait_send()
+    for d, t, copy in yr:
+        if d:
+            copy.wait_send()
+        else:
+            pl.when(t != r)(copy.wait_send)
 
 
 def update(a_ref, left_ref, right_ref, w_ref, out_ref, companion_ref):
@@ -239,7 +266,8 @@
     nr, nc = lax.axis_size("row"), lax.axis_size("col")
     _, b, n = reflectors.shape
     m, k = matrix.shape
-    ratio, h = nr // nc, b // nc
+    ratio, h, hr = nr // nc, b // nc, b // nr
+    wide = pl.cdiv(n, 128) * 128
     f32 = jnp.float32
     dma = pltpu.SemaphoreType.DMA
     vmem = pl.BlockSpec(memory_space=pltpu.VMEM)
@@ -257,27 +285,25 @@
         in_specs=[hbm, hbm, hbm],
         out_specs=(vmem,) * 4,
         scratch_shapes=[
-            pltpu.VMEM((m, k), jnp.bfloat16),
-            pltpu.VMEM((m, k), jnp.bfloat16),
             pltpu.VMEM((nc, h, n), f32),
             pltpu.VMEM((b, b), f32),
-            pltpu.VMEM((slots, h, n), f32),
-            pltpu.VMEM((nc, h, n + b), f32),
-            pltpu.VMEM((nc, h, n + b), f32),
-            pltpu.VMEM((h, n), f32),
-            pltpu.VMEM((slots, h, n), f32),
-            pltpu.VMEM((nc, h, n), f32),
-            pltpu.VMEM((nr, h, b), f32),
-            pltpu.VMEM((h, b), f32),
-            pltpu.VMEM((h, b), f32),
-            pltpu.VMEM((nc, h, b), f32),
+            pltpu.VMEM((h, wide), f32),
+            pltpu.VMEM((slots, h, wide), f32),
+            pltpu.VMEM((nr, hr, k), f32),
+            pltpu.VMEM((nr, hr, k), f32),
+            pltpu.VMEM((nr, hr, k), f32),
+            pltpu.VMEM((ratio, hr, wide), f32),
+            pltpu.VMEM((nr, hr, wide), f32),
+            pltpu.VMEM((hr, 128), f32),
+            pltpu.VMEM((nc, hr, 128), f32),
+            pltpu.VMEM((nr, hr, 128), f32),
             dma((3,)),
             dma((sends,)), dma((slots,)),
-            dma((nc - 1,)), dma((nc,)),
-            dma((sends,)), dma((slots,)),
+            dma((nr - 1,)), dma((nr,)),
+            dma((nr - 1,)), dma((nr,)),
+            dma((nc, ratio)), dma((nr,)),
             dma((nc - 1,)), dma((nc,)),
             dma((nr - 1,)), dma((nr,)),
-            dma((nc - 1,)), dma((nc,)),
         ],
         compiler_params=pltpu.CompilerParams(
             collective_id=0, has_side_effects=True, vmem_limit_bytes=32 * 1024 * 1024

time: 33.2 us -> 34.8 us (1.048)
  Pallas kernels: 32.4 us -> 34 us
    pallas_call x1, Pallas kernels: 30 us -> 31.5 us  [shards(): pl.pallas_call(functools.partial(kernel, nr, nc), out_shape=(jax.ShapeDty...]
where the time goes in v2:
time: 34.8 us; the launch traced here: 34.6 us
  Pallas kernels  34 us (98%)
  between operations  0.64 us (2%)
    pallas_call x1, Pallas kernels, shards(): pl.pallas_call(functools.partial(kernel, nr, nc), out_shape=(jax.ShapeDty...  31.5 us
    pallas_call x1, Pallas kernels, shards(): pl.pallas_call(update, grid=(steps,), out_shape=(jax.ShapeDtypeStruct((m,...  2.46 us

profile of v2, /device:TPU:0, one launch (start us, length us, event | category | flops | bytes accessed | tf_op | source)
XLA Modules:
  0.0 34.6 jit_solution(10630685575189973956)
XLA Ops:
  0.6 31.5 %reflector_update.1 = (f32[448,896]{1,0:T(8,128)S(1)}, bf16[448,384]{1,0:T(8,128)(2,1)S(1)}, bf16[384,896]{1,0:T(8,128)(2,1)S(1)}, f32[1,64,448]{2,1,0:T(8,128)S(1)}) custom-call(f32[4,16,448]{2,1,0:T(8,128)} %bitcast.2, f32[448,896]{1,0:T(8,128)} %a_hbm.1, f32[64,64]{1,0:T(8,128)} %bitcast.3), custom_call_target="tpu_custom_call" | custom-call | tf_op jit(solution)/shard_map/reflector_update/pallas_call | solution.py:277
  32.2 2.5 %tile_update.1 = (f32[448,896]{1,0:T(8,128)}, f32[1,64,448]{2,1,0:T(8,128)}) custom-call(f32[448,896]{1,0:T(8,128)S(1)} %get-tuple-element.6.a_ref, bf16[448,384]{1,0:T(8,128)(2,1)S(1)} %get-tuple-element.7.left_ref, bf16[384,896]{1,0:T(8,128)(2,1)S(1)} %get-tuple-element.8.right_ref, f32[1,64,448]{2,1,0:T(8,128)S(1)} %get-tuple-element.9.w_ref), custom_call_target="tpu_custom_call" | custom-call | tf_op jit(solution)/shard_map/tile_update/pallas_call | solution.py:314

commit v3 on v1

--- a/solution.py
+++ b/solution.py
@@ -25,9 +25,13 @@
     return dot(ah, bh, da, db) + (dot(ah, bl, da, db) + dot(al, bh, da, db))
 
 
+def wrap(x, size):
+    return jnp.where(x >= size, x - size, x)
+
+
 def kernel(
     nr, nc, v_hbm, a_hbm, f_hbm, a_ref, left_ref, right_ref, w_ref,
-    a_hi, a_lo, v_ref, f_ref, vrecv, pbuf, precv, yown, yrecv, yrow, srow, spart, sown, sfull,
+    a_hi, a_lo, v_ref, f_ref, vown, vrecv, pbuf, precv, yown, yrecv, yrow, srow, spart, sown, sfull,
     in_sem, gv_send, gv_recv, rs_send, rs_recv, gy_send, gy_recv, yr_send, yr_recv, sr_send, sr_recv, sc_send, sc_recv,
 ):
     ratio, half = nr // nc, nc // 2
@@ -35,7 +39,7 @@
     g, i = r // ratio, r % ratio
     line, core = c // 2, c % 2
     aligned = g % 2 == core
-    n = v_ref.shape[2]
+    n = v_hbm.shape[2]
     b = f_ref.shape[0]
     h = b // nc
 
@@ -51,8 +55,8 @@
             src_ref=src, dst_ref=dst, send_sem=send, recv_sem=recv, device_id=(row, col), device_id_type=MESH
         )
 
-    row_peers = [lax.rem(r + k, nr) for k in range(1, nr)]
-    col_peers = [lax.rem(c + k, nc) for k in range(1, nc)]
+    row_peers = [wrap(r + k, nr) for k in range(1, nr)]
+    col_peers = [wrap(c + k, nc) for k in range(1, nc)]
 
     def signal(row, col):
         pl.semaphore_signal(barrier, inc=1, device_id=(row, col), device_id_type=MESH)
@@ -65,11 +69,11 @@
     for d in range(ratio):
         for e in range(half):
             if d or e:
-                signal(g * ratio + lax.rem(i + d, ratio), lax.rem(line + e, half) * 2 + core)
+                signal(g * ratio + wrap(i + d, ratio), wrap(line + e, half) * 2 + core)
     for j in range(half):
         for e in range(2):
-            row = (lax.rem(g // 2 + j, half) * 2 + core) * ratio + i
-            col = line * 2 + lax.rem(core + e, 2)
+            row = (wrap(g // 2 + j, half) * 2 + core) * ratio + i
+            col = line * 2 + wrap(core + e, 2)
             if j or e:
                 signal(row, col)
             else:
@@ -86,7 +90,7 @@
             self.first = [
                 remote(
                     src, buf.at[slot], send.at[j], recv.at[slot],
-                    lax.rem(g + j, nc) * ratio + i, line * 2 + g % 2,
+                    wrap(g + j, nc) * ratio + i, line * 2 + g % 2,
                 )
                 for j in range(nc)
             ]
@@ -102,7 +106,7 @@
             self.second = []
             k = nc
             for j in list(range(1, half)) + [0]:
-                a = lax.rem(line + j, half)
+                a = wrap(line + j, half)
                 for e in range(2):
                     final = i * nc + line * 2 + e
                     slot = relay + a * 2 + e if j else final
@@ -112,7 +116,7 @@
                     for d in range(0 if j else 1, ratio):
                         copy = remote(
                             self.buf.at[slot], self.buf.at[final], self.send.at[k], self.recv.at[final],
-                            g * ratio + lax.rem(i + d, ratio), a * 2 + core,
+                            g * ratio + wrap(i + d, ratio), a * 2 + core,
                         )
                         copy.start()
                         self.second.append(copy)
@@ -123,7 +127,7 @@
                 for e in range(half):
                     for k in range(2):
                         if d or e:
-                            slot = lax.rem(i + d, ratio) * nc + lax.rem(line + e, half) * 2 + k
+                            slot = wrap(i + d, ratio) * nc + wrap(line + e, half) * 2 + k
                             remote(
                                 self.src, self.buf.at[slot], self.send.at[0], self.recv.at[slot], r, c
                             ).wait_recv()
@@ -131,7 +135,7 @@
         def columns(self):
             return jnp.concatenate(
                 [
-                    jnp.concatenate([self.buf[t * nc + q] for q in range(nc)], axis=0)
+                    jnp.concatenate([self.buf[t * nc + q, :, :n] for q in range(nc)], axis=0)
                     for t in range(ratio)
                 ],
                 axis=1,
@@ -142,9 +146,10 @@
             for copy in self.first[1:] + self.second:
                 copy.wait_send()
 
-    gv = Gather(v_hbm.at[c], vrecv, gv_send, gv_recv)
     v_copy.wait()
-    gv.forward(v_ref.at[c])
+    vown[:, :n] = v_ref[c]
+    gv = Gather(vown, vrecv, gv_send, gv_recv)
+    gv.forward(vown)
 
     f_copy.wait()
     a_copy.wait()
@@ -170,9 +175,9 @@
     for k, q in enumerate(col_peers):
         remote(pbuf.at[q], precv.at[q], rs_send.at[k], rs_recv.at[q], r, q).wait_recv()
         total = total + precv[q]
-    yown[...] = total[:, :n]
-    spart[...] = total[:, n:]
-    srow[r] = total[:, n:]
+    yown[...] = total
+    spart[:, :b] = total[:, n:]
+    srow[r, :, :b] = total[:, n:]
 
     sr = [remote(spart, srow.at[r], sr_send.at[k], sr_recv.at[r], t, c) for k, t in enumerate(row_peers)]
     for copy in sr:
@@ -198,11 +203,11 @@
     factor = f_ref[...]
     for k, q in enumerate(col_peers):
         remote(yown, yrow.at[q], yr_send.at[k], yr_recv.at[q], r, q).wait_recv()
-    y_rows = jnp.concatenate([yrow[q] for q in range(nc)], axis=0)
+    y_rows = jnp.concatenate([yrow[q, :, :n] for q in range(nc)], axis=0)
     x_rows = dot3(factor, y_rows, 0, 0)
     for k, q in enumerate(col_peers):
         remote(sown, sfull.at[q], sc_send.at[k], sc_recv.at[q], r, q).wait_recv()
-    square = jnp.concatenate([sfull[q] for q in range(nc)], axis=0)
+    square = jnp.concatenate([sfull[q, :, :b] for q in range(nc)], axis=0)
     mixing = 0.5 * dot3(dot3(square, factor, 1, 0), factor, 0, 0)
     w_rows = x_rows - dot3(mixing, v_rows, 1, 0)
     w_ref[0] = w_rows
@@ -261,16 +266,17 @@
             pltpu.VMEM((m, k), jnp.bfloat16),
             pltpu.VMEM((nc, h, n), f32),
             pltpu.VMEM((b, b), f32),
-            pltpu.VMEM((slots, h, n), f32),
+            pltpu.VMEM((h, n + b), f32),
+            pltpu.VMEM((slots, h, n + b), f32),
             pltpu.VMEM((nc, h, n + b), f32),
             pltpu.VMEM((nc, h, n + b), f32),
-            pltpu.VMEM((h, n), f32),
-            pltpu.VMEM((slots, h, n), f32),
-            pltpu.VMEM((nc, h, n), f32),
-            pltpu.VMEM((nr, h, b), f32),
-            pltpu.VMEM((h, b), f32),
-            pltpu.VMEM((h, b), f32),
-            pltpu.VMEM((nc, h, b), f32),
+            pltpu.VMEM((h, n + b), f32),
+            pltpu.VMEM((slots, h, n + b), f32),
+            pltpu.VMEM((nc, h, n + b), f32),
+            pltpu.VMEM((nr, h, 2 * b), f32),
+            pltpu.VMEM((h, 2 * b), f32),
+            pltpu.VMEM((h, 2 * b), f32),
+            pltpu.VMEM((nc, h, 2 * b), f32),
             dma((3,)),
             dma((sends,)), dma((slots,)),
             dma((nc - 1,)), dma((nc,)),
@@ -284,7 +290,7 @@
         ),
         name="reflector_update",
     )(*(pltpu.with_memory_space_constraint(x, pltpu.HBM) for x in (reflectors.reshape(nc, h, n), matrix, factors[0])))
-    steps = 4
+    steps = 2
     return pl.pallas_call(
         update,
         grid=(steps,),

time: 33.2 us -> 32.3 us (0.973)
  Pallas kernels: 32.4 us -> 31.5 us
    pallas_call x1, Pallas kernels: 2.46 us -> 1.73 us  [shards(): pl.pallas_call(update, grid=(steps,), out_shape=(jax.ShapeDtypeStruct((m,...]
where the time goes in v3:
time: 32.3 us; the launch traced here: 32.1 us
  Pallas kernels  31.5 us (98%)
  between operations  0.64 us (2%)
    pallas_call x1, Pallas kernels, shards(): pl.pallas_call(functools.partial(kernel, nr, nc), out_shape=(jax.ShapeDty...  29.7 us
    pallas_call x1, Pallas kernels, shards(): pl.pallas_call(update, grid=(steps,), out_shape=(jax.ShapeDtypeStruct((m,...  1.73 us

profile of v3, /device:TPU:0, one launch (start us, length us, event | category | flops | bytes accessed | tf_op | source)
XLA Modules:
  0.0 32.1 jit_solution(17944950529846128338)
XLA Ops:
  0.6 29.7 %reflector_update.1 = (f32[448,896]{1,0:T(8,128)S(1)}, bf16[448,384]{1,0:T(8,128)(2,1)S(1)}, bf16[384,896]{1,0:T(8,128)(2,1)S(1)}, f32[1,64,448]{2,1,0:T(8,128)S(1)}) custom-call(f32[4,16,448]{2,1,0:T(8,128)} %bitcast.2, f32[448,896]{1,0:T(8,128)} %a_hbm.1, f32[64,64]{1,0:T(8,128)} %bitcast.3), custom_call_target="tpu_custom_call" | custom-call | tf_op jit(solution)/shard_map/reflector_update/pallas_call | solution.py:254
  30.4 1.7 %tile_update.1 = (f32[448,896]{1,0:T(8,128)}, f32[1,64,448]{2,1,0:T(8,128)}) custom-call(f32[448,896]{1,0:T(8,128)S(1)} %get-tuple-element.6.a_ref, bf16[448,384]{1,0:T(8,128)(2,1)S(1)} %get-tuple-element.7.left_ref, bf16[384,896]{1,0:T(8,128)(2,1)S(1)} %get-tuple-element.8.right_ref, f32[1,64,448]{2,1,0:T(8,128)S(1)} %get-tuple-element.9.w_ref), custom_call_target="tpu_custom_call" | custom-call | tf_op jit(solution)/shard_map/tile_update/pallas_call | solution.py:294

commit v4 on v3

--- a/solution.py
+++ b/solution.py
@@ -34,11 +34,10 @@
     a_hi, a_lo, v_ref, f_ref, vown, vrecv, pbuf, precv, yown, yrecv, yrow, srow, spart, sown, sfull,
     in_sem, gv_send, gv_recv, rs_send, rs_recv, gy_send, gy_recv, yr_send, yr_recv, sr_send, sr_recv, sc_send, sc_recv,
 ):
-    ratio, half = nr // nc, nc // 2
+    ratio = nr // nc
     r, c = lax.axis_index("row"), lax.axis_index("col")
-    g, i = r // ratio, r % ratio
-    line, core = c // 2, c % 2
-    aligned = g % 2 == core
+    home, i = r // ratio, r % ratio
+    at_home = home == c
     n = v_hbm.shape[2]
     b = f_ref.shape[0]
     h = b // nc
@@ -66,90 +65,49 @@
         signal(t, c)
     for q in col_peers:
         signal(r, q)
-    for d in range(ratio):
-        for e in range(half):
-            if d or e:
-                signal(g * ratio + wrap(i + d, ratio), wrap(line + e, half) * 2 + core)
-    for j in range(half):
-        for e in range(2):
-            row = (wrap(g // 2 + j, half) * 2 + core) * ratio + i
-            col = line * 2 + wrap(core + e, 2)
-            if j or e:
-                signal(row, col)
-            else:
-                pl.when(jnp.logical_not(aligned))(functools.partial(signal, row, col))
-    count = nr - 1 + nc - 1 + ratio * half - 1 + nc
-    pl.semaphore_wait(barrier, count - jnp.where(aligned, 1, 0))
-
-    relay = ratio * nc
+    for q in col_peers:
+        for e in range(ratio):
+            signal(c * ratio + e, q)
+    pl.semaphore_wait(barrier, nr - 1 + nc - 1 + jnp.where(at_home, 0, nr))
 
     class Gather:
         def __init__(self, src, buf, send, recv):
             self.src, self.buf, self.send, self.recv = src, buf, send, recv
-            self.slot = slot = jnp.where(g // 2 == line, i * nc + c, relay + (g // 2) * 2 + core)
-            self.first = [
-                remote(
-                    src, buf.at[slot], send.at[j], recv.at[slot],
-                    wrap(g + j, nc) * ratio + i, line * 2 + g % 2,
-                )
-                for j in range(nc)
+            self.copies = [
+                remote(src, buf.at[i, c], send.at[k], recv.at[i, c], wrap(r + k, nr), home) for k in range(nr)
             ]
-            for copy in self.first[1:]:
+            for copy in self.copies[1:]:
                 copy.start()
-            pl.when(jnp.logical_not(aligned))(self.first[0].start)
-
-        def forward(self, own):
-            @pl.when(aligned)
+            pl.when(jnp.logical_not(at_home))(self.copies[0].start)
+
+            @pl.when(at_home)
             def _():
-                self.buf[self.slot] = own[...]
-
-            self.second = []
-            k = nc
-            for j in list(range(1, half)) + [0]:
-                a = wrap(line + j, half)
-                for e in range(2):
-                    final = i * nc + line * 2 + e
-                    slot = relay + a * 2 + e if j else final
-                    mine = jnp.logical_and(a * 2 + core == g, e == core)
-                    arrival = remote(self.src, self.buf.at[slot], self.send.at[0], self.recv.at[slot], r, c)
-                    pl.when(jnp.logical_not(mine))(arrival.wait_recv)
-                    for d in range(0 if j else 1, ratio):
-                        copy = remote(
-                            self.buf.at[slot], self.buf.at[final], self.send.at[k], self.recv.at[final],
-                            g * ratio + wrap(i + d, ratio), a * 2 + core,
-                        )
-                        copy.start()
-                        self.second.append(copy)
-                        k += 1
+                buf[i, c] = src[...]
 
         def wait(self):
-            for d in range(ratio):
-                for e in range(half):
-                    for k in range(2):
-                        if d or e:
-                            slot = wrap(i + d, ratio) * nc + wrap(line + e, half) * 2 + k
-                            remote(
-                                self.src, self.buf.at[slot], self.send.at[0], self.recv.at[slot], r, c
-                            ).wait_recv()
+            for j in range(nc):
+                q = wrap(c + j, nc)
+                for e in range(ratio):
+                    arrival = remote(self.src, self.buf.at[e, q], self.send.at[0], self.recv.at[e, q], r, c)
+                    if j:
+                        arrival.wait_recv()
+                    else:
+                        pl.when(c * ratio + e != r)(arrival.wait_recv)
 
         def columns(self):
             return jnp.concatenate(
-                [
-                    jnp.concatenate([self.buf[t * nc + q, :, :n] for q in range(nc)], axis=0)
-                    for t in range(ratio)
-                ],
+                [jnp.concatenate([self.buf[t, q, :, :n] for q in range(nc)], axis=0) for t in range(ratio)],
                 axis=1,
             )
 
         def end(self):
-            pl.when(jnp.logical_not(aligned))(self.first[0].wait_send)
-            for copy in self.first[1:] + self.second:
+            pl.when(jnp.logical_not(at_home))(self.copies[0].wait_send)
+            for copy in self.copies[1:]:
                 copy.wait_send()
 
     v_copy.wait()
     vown[:, :n] = v_ref[c]
     gv = Gather(vown, vrecv, gv_send, gv_recv)
-    gv.forward(vown)
 
     f_copy.wait()
     a_copy.wait()
@@ -198,7 +156,6 @@
     sc = [remote(sown, sfull.at[c], sc_send.at[k], sc_recv.at[c], r, q) for k, q in enumerate(col_peers)]
     for copy in sc:
         copy.start()
-    gy.forward(yown)
 
     factor = f_ref[...]
     for k, q in enumerate(col_peers):
@@ -249,8 +206,6 @@
     dma = pltpu.SemaphoreType.DMA
     vmem = pl.BlockSpec(memory_space=pltpu.VMEM)
     hbm = pl.BlockSpec(memory_space=pltpu.HBM)
-    slots = ratio * nc + nc
-    sends = nc + 2 * (ratio * (nc // 2) - 1)
     held = pl.pallas_call(
         functools.partial(kernel, nr, nc),
         out_shape=(
@@ -267,20 +222,20 @@
             pltpu.VMEM((nc, h, n), f32),
             pltpu.VMEM((b, b), f32),
             pltpu.VMEM((h, n + b), f32),
-            pltpu.VMEM((slots, h, n + b), f32),
+            pltpu.VMEM((ratio, nc, h, n + b), f32),
             pltpu.VMEM((nc, h, n + b), f32),
             pltpu.VMEM((nc, h, n + b), f32),
             pltpu.VMEM((h, n + b), f32),
-            pltpu.VMEM((slots, h, n + b), f32),
+            pltpu.VMEM((ratio, nc, h, n + b), f32),
             pltpu.VMEM((nc, h, n + b), f32),
             pltpu.VMEM((nr, h, 2 * b), f32),
             pltpu.VMEM((h, 2 * b), f32),
             pltpu.VMEM((h, 2 * b), f32),
             pltpu.VMEM((nc, h, 2 * b), f32),
             dma((3,)),
-            dma((sends,)), dma((slots,)),
+            dma((nr,)), dma((ratio, nc)),
             dma((nc - 1,)), dma((nc,)),
-            dma((sends,)), dma((slots,)),
+            dma((nr,)), dma((ratio, nc)),
             dma((nc - 1,)), dma((nc,)),
             dma((nr - 1,)), dma((nr,)),
             dma((nc - 1,)), dma((nc,)),

time: 32.3 us -> 31.5 us (0.975)
  Pallas kernels: 31.5 us -> 30.7 us
    pallas_call x1, Pallas kernels: 29.7 us -> 29 us  [shards(): pl.pallas_call(functools.partial(kernel, nr, nc), out_shape=(jax.ShapeDty...]
where the time goes in v4:
time: 31.5 us; the launch traced here: 31.4 us
  Pallas kernels  30.7 us (97%)
  between operations  0.64 us (2%)
    pallas_call x1, Pallas kernels, shards(): pl.pallas_call(functools.partial(kernel, nr, nc), out_shape=(jax.ShapeDty...  29 us
    pallas_call x1, Pallas kernels, shards(): pl.pallas_call(update, grid=(steps,), out_shape=(jax.ShapeDtypeStruct((m,...  1.73 us

profile of v4, /device:TPU:0, one launch (start us, length us, event | category | flops | bytes accessed | tf_op | source)
XLA Modules:
  0.0 31.4 jit_solution(11223848174820958957)
XLA Ops:
  0.6 29.0 %reflector_update.1 = (f32[448,896]{1,0:T(8,128)S(1)}, bf16[448,384]{1,0:T(8,128)(2,1)S(1)}, bf16[384,896]{1,0:T(8,128)(2,1)S(1)}, f32[1,64,448]{2,1,0:T(8,128)S(1)}) custom-call(f32[4,16,448]{2,1,0:T(8,128)} %bitcast.2, f32[448,896]{1,0:T(8,128)} %a_hbm.1, f32[64,64]{1,0:T(8,128)} %bitcast.3), custom_call_target="tpu_custom_call" | custom-call | tf_op jit(solution)/shard_map/reflector_update/pallas_call | solution.py:209
  29.7 1.7 %tile_update.1 = (f32[448,896]{1,0:T(8,128)}, f32[1,64,448]{2,1,0:T(8,128)}) custom-call(f32[448,896]{1,0:T(8,128)S(1)} %get-tuple-element.6.a_ref, bf16[448,384]{1,0:T(8,128)(2,1)S(1)} %get-tuple-element.7.left_ref, bf16[384,896]{1,0:T(8,128)(2,1)S(1)} %get-tuple-element.8.right_ref, f32[1,64,448]{2,1,0:T(8,128)S(1)} %get-tuple-element.9.w_ref), custom_call_target="tpu_custom_call" | custom-call | tf_op jit(solution)/shard_map/tile_update/pallas_call | solution.py:249

commit v5 on v4

--- a/solution.py
+++ b/solution.py
@@ -31,7 +31,7 @@
 
 def kernel(
     nr, nc, v_hbm, a_hbm, f_hbm, a_ref, left_ref, right_ref, w_ref,
-    a_hi, a_lo, v_ref, f_ref, vown, vrecv, pbuf, precv, yown, yrecv, yrow, srow, spart, sown, sfull,
+    a_hi, a_lo, v_ref, f_ref, vrecv, pbuf, precv, yown, yrecv, yrow, srow, spart, sown, sfull,
     in_sem, gv_send, gv_recv, rs_send, rs_recv, gy_send, gy_recv, yr_send, yr_recv, sr_send, sr_recv, sc_send, sc_recv,
 ):
     ratio = nr // nc
@@ -94,20 +94,31 @@
                     else:
                         pl.when(c * ratio + e != r)(arrival.wait_recv)
 
-        def columns(self):
-            return jnp.concatenate(
-                [jnp.concatenate([self.buf[t, q, :, :n] for q in range(nc)], axis=0) for t in range(ratio)],
-                axis=1,
-            )
-
         def end(self):
             pl.when(jnp.logical_not(at_home))(self.copies[0].wait_send)
             for copy in self.copies[1:]:
                 copy.wait_send()
 
+    def columns(buf):
+        return jnp.concatenate(
+            [jnp.concatenate([buf[t, q, :, :n] for q in range(nc)], axis=0) for t in range(ratio)], axis=1
+        )
+
+    def unless(own, action):
+        pl.when(jnp.logical_not(own))(action)
+
     v_copy.wait()
-    vown[:, :n] = v_ref[c]
-    gv = Gather(vown, vrecv, gv_send, gv_recv)
+    gv = []
+    for e in range(ratio):
+        t = c + e * nc
+        copy = remote(v_ref, vrecv.at[i], gv_send.at[e], gv_recv.at[i], t, home)
+        own = jnp.logical_and(at_home, t == r)
+        unless(own, copy.start)
+        gv.append((own, copy))
+
+        @pl.when(own)
+        def _():
+            vrecv[i] = v_ref[...]
 
     f_copy.wait()
     a_copy.wait()
@@ -115,27 +126,36 @@
     a_hi[...] = hi
     a_lo[...] = lo
     v_rows = jnp.concatenate([v_ref[q] for q in range(nc)], axis=0)
-
-    gv.wait()
-    v_cols = gv.columns()
+    rh, rl = split(v_rows.T)
+
+    helper = lax.rem(r, nc)
+    for e in range(ratio):
+        own = jnp.logical_and(c * ratio + e == r, helper == c)
+        unless(own, remote(v_ref, vrecv.at[e], gv_send.at[e], gv_recv.at[e], c * ratio + e, helper).wait_recv)
+    v_cols = columns(vrecv)
     vh, vl = split(v_cols)
     both = dot(jnp.concatenate([vh, vl], axis=0), a_hi[...], 1, 1)
     partial = both[:b] + (both[b:] + dot(vh, a_lo[...], 1, 1))
-    term = dot3(v_rows, partial, 1, 1)
     for q in range(nc):
         pbuf[q, :, :n] = partial[q * h:(q + 1) * h]
-        pbuf[q, :, n:] = term[q * h:(q + 1) * h]
 
     rs = [remote(pbuf.at[q], precv.at[c], rs_send.at[k], rs_recv.at[c], r, q) for k, q in enumerate(col_peers)]
     for copy in rs:
         copy.start()
+    right_ref[b:2 * b] = vh
+    right_ref[3 * b:4 * b] = vl
+    right_ref[5 * b:] = vh
+    left_ref[:, :b] = rh
+    left_ref[:, 2 * b:3 * b] = rh
+    left_ref[:, 4 * b:5 * b] = rl
     total = pbuf[c]
     for k, q in enumerate(col_peers):
         remote(pbuf.at[q], precv.at[q], rs_send.at[k], rs_recv.at[q], r, q).wait_recv()
         total = total + precv[q]
     yown[...] = total
-    spart[:, :b] = total[:, n:]
-    srow[r, :, :b] = total[:, n:]
+    term = dot3(total[:, :n], v_rows, 1, 1)
+    spart[:, :b] = term
+    srow[r, :, :b] = term
 
     sr = [remote(spart, srow.at[r], sr_send.at[k], sr_recv.at[r], t, c) for k, t in enumerate(row_peers)]
     for copy in sr:
@@ -165,26 +185,25 @@
     for k, q in enumerate(col_peers):
         remote(sown, sfull.at[q], sc_send.at[k], sc_recv.at[q], r, q).wait_recv()
     square = jnp.concatenate([sfull[q, :, :b] for q in range(nc)], axis=0)
-    mixing = 0.5 * dot3(dot3(square, factor, 1, 0), factor, 0, 0)
+    mixing = 0.5 * dot3(factor, dot3(square, factor, 1, 0), 0, 0)
     w_rows = x_rows - dot3(mixing, v_rows, 1, 0)
     w_ref[0] = w_rows
-    lh, ll = split(jnp.concatenate([v_rows, w_rows], axis=0).T)
-    left_ref[...] = jnp.concatenate([lh, lh, ll], axis=1)
-    right_ref[b:2 * b] = vh
-    right_ref[3 * b:4 * b] = vl
-    right_ref[5 * b:] = vh
+    lh, ll = split(w_rows.T)
+    left_ref[:, b:2 * b] = lh
+    left_ref[:, 3 * b:4 * b] = lh
+    left_ref[:, 5 * b:] = ll
     mixed = dot3(mixing, v_cols, 1, 0)
+    for own, copy in gv:
+        unless(own, copy.wait_send)
+    gy.end()
+    for copy in rs + sr + yr + sc:
+        copy.wait_send()
 
     gy.wait()
-    wh, wl = split(dot3(factor, gy.columns(), 0, 0) - mixed)
+    wh, wl = split(dot3(factor, columns(yrecv), 0, 0) - mixed)
     right_ref[:b] = wh
     right_ref[2 * b:3 * b] = wl
     right_ref[4 * b:5 * b] = wh
-
-    gv.end()
-    gy.end()
-    for copy in rs + sr + yr + sc:
-        copy.wait_send()
 
 
 def update(a_ref, left_ref, right_ref, w_ref, out_ref, companion_ref):
@@ -202,6 +221,7 @@
     _, b, n = reflectors.shape
     m, k = matrix.shape
     ratio, h = nr // nc, b // nc
+    wide = pl.cdiv(n, 128) * 128
     f32 = jnp.float32
     dma = pltpu.SemaphoreType.DMA
     vmem = pl.BlockSpec(memory_space=pltpu.VMEM)
@@ -221,19 +241,18 @@
             pltpu.VMEM((m, k), jnp.bfloat16),
             pltpu.VMEM((nc, h, n), f32),
             pltpu.VMEM((b, b), f32),
-            pltpu.VMEM((h, n + b), f32),
-            pltpu.VMEM((ratio, nc, h, n + b), f32),
-            pltpu.VMEM((nc, h, n + b), f32),
-            pltpu.VMEM((nc, h, n + b), f32),
-            pltpu.VMEM((h, n + b), f32),
-            pltpu.VMEM((ratio, nc, h, n + b), f32),
-            pltpu.VMEM((nc, h, n + b), f32),
+            pltpu.VMEM((ratio, nc, h, n), f32),
+            pltpu.VMEM((nc, h, wide), f32),
+            pltpu.VMEM((nc, h, wide), f32),
+            pltpu.VMEM((h, wide), f32),
+            pltpu.VMEM((ratio, nc, h, wide), f32),
+            pltpu.VMEM((nc, h, wide), f32),
             pltpu.VMEM((nr, h, 2 * b), f32),
             pltpu.VMEM((h, 2 * b), f32),
             pltpu.VMEM((h, 2 * b), f32),
             pltpu.VMEM((nc, h, 2 * b), f32),
             dma((3,)),
-            dma((nr,)), dma((ratio, nc)),
+            dma((ratio,)), dma((ratio,)),
             dma((nc - 1,)), dma((nc,)),
             dma((nr,)), dma((ratio, nc)),
             dma((nc - 1,)), dma((nc,)),

time: 31.5 us -> 30.4 us (0.965)
  Pallas kernels: 30.7 us -> 29.7 us
    pallas_call x1, Pallas kernels: 29 us -> 27.9 us  [shards(): pl.pallas_call(functools.partial(kernel, nr, nc), out_shape=(jax.ShapeDty...]
where the time goes in v5:
time: 30.4 us; the launch traced here: 30.3 us
  Pallas kernels  29.7 us (98%)
  between operations  0.64 us (2%)
    pallas_call x1, Pallas kernels, shards(): pl.pallas_call(functools.partial(kernel, nr, nc), out_shape=(jax.ShapeDty...  27.9 us
    pallas_call x1, Pallas kernels, shards(): pl.pallas_call(update, grid=(steps,), out_shape=(jax.ShapeDtypeStruct((m,...  1.73 us

profile of v5, /device:TPU:0, one launch (start us, length us, event | category | flops | bytes accessed | tf_op | source)
XLA Modules:
  0.0 30.3 jit_solution(13924137593165304343)
XLA Ops:
  0.6 27.9 %reflector_update.1 = (f32[448,896]{1,0:T(8,128)S(1)}, bf16[448,384]{1,0:T(8,128)(2,1)S(1)}, bf16[384,896]{1,0:T(8,128)(2,1)S(1)}, f32[1,64,448]{2,1,0:T(8,128)S(1)}) custom-call(f32[4,16,448]{2,1,0:T(8,128)} %bitcast.2, f32[448,896]{1,0:T(8,128)} %a_hbm.1, f32[64,64]{1,0:T(8,128)} %bitcast.3), custom_call_target="tpu_custom_call" | custom-call | tf_op jit(solution)/shard_map/reflector_update/pallas_call | solution.py:229
  28.6 1.7 %tile_update.1 = (f32[448,896]{1,0:T(8,128)}, f32[1,64,448]{2,1,0:T(8,128)}) custom-call(f32[448,896]{1,0:T(8,128)S(1)} %get-tuple-element.6.a_ref, bf16[448,384]{1,0:T(8,128)(2,1)S(1)} %get-tuple-element.7.left_ref, bf16[384,896]{1,0:T(8,128)(2,1)S(1)} %get-tuple-element.8.right_ref, f32[1,64,448]{2,1,0:T(8,128)S(1)} %get-tuple-element.9.w_ref), custom_call_target="tpu_custom_call" | custom-call | tf_op jit(solution)/shard_map/tile_update/pallas_call | solution.py:268

commit v6 on v5

--- a/solution.py
+++ b/solution.py
@@ -122,7 +122,7 @@
 
     f_copy.wait()
     a_copy.wait()
-    hi, lo = split(a_ref[...])
+    hi, lo = split(a_ref[...].T)
     a_hi[...] = hi
     a_lo[...] = lo
     v_rows = jnp.concatenate([v_ref[q] for q in range(nc)], axis=0)
@@ -134,8 +134,8 @@
         unless(own, remote(v_ref, vrecv.at[e], gv_send.at[e], gv_recv.at[e], c * ratio + e, helper).wait_recv)
     v_cols = columns(vrecv)
     vh, vl = split(v_cols)
-    both = dot(jnp.concatenate([vh, vl], axis=0), a_hi[...], 1, 1)
-    partial = both[:b] + (both[b:] + dot(vh, a_lo[...], 1, 1))
+    both = dot(jnp.concatenate([vh, vl], axis=0), a_hi[...], 1, 0)
+    partial = both[:b] + (both[b:] + dot(vh, a_lo[...], 1, 0))
     for q in range(nc):
         pbuf[q, :, :n] = partial[q * h:(q + 1) * h]
 
@@ -237,8 +237,8 @@
         in_specs=[hbm, hbm, hbm],
         out_specs=(vmem,) * 4,
         scratch_shapes=[
-            pltpu.VMEM((m, k), jnp.bfloat16),
-            pltpu.VMEM((m, k), jnp.bfloat16),
+            pltpu.VMEM((k, m), jnp.bfloat16),
+            pltpu.VMEM((k, m), jnp.bfloat16),
             pltpu.VMEM((nc, h, n), f32),
             pltpu.VMEM((b, b), f32),
             pltpu.VMEM((ratio, nc, h, n), f32),

time: 30.4 us -> 30.2 us (level)
  no operation moved by 1% of the time
where the time goes in v6:
time: 30.2 us; the launch traced here: 30 us
  Pallas kernels  29.4 us (97%)
  between operations  0.64 us (2%)
    pallas_call x1, Pallas kernels, shards(): pl.pallas_call(functools.partial(kernel, nr, nc), out_shape=(jax.ShapeDty...  27.6 us
    pallas_call x1, Pallas kernels, shards(): pl.pallas_call(update, grid=(steps,), out_shape=(jax.ShapeDtypeStruct((m,...  1.73 us

profile of v6, /device:TPU:0, one launch (start us, length us, event | category | flops | bytes accessed | tf_op | source)
XLA Modules:
  0.0 30.0 jit_solution(8254344088281583088)
XLA Ops:
  0.6 27.6 %reflector_update.1 = (f32[448,896]{1,0:T(8,128)S(1)}, bf16[448,384]{1,0:T(8,128)(2,1)S(1)}, bf16[384,896]{1,0:T(8,128)(2,1)S(1)}, f32[1,64,448]{2,1,0:T(8,128)S(1)}) custom-call(f32[4,16,448]{2,1,0:T(8,128)} %bitcast.2, f32[448,896]{1,0:T(8,128)} %a_hbm.1, f32[64,64]{1,0:T(8,128)} %bitcast.3), custom_call_target="tpu_custom_call" | custom-call | tf_op jit(solution)/shard_map/reflector_update/pallas_call | solution.py:229
  28.3 1.7 %tile_update.1 = (f32[448,896]{1,0:T(8,128)}, f32[1,64,448]{2,1,0:T(8,128)}) custom-call(f32[448,896]{1,0:T(8,128)S(1)} %get-tuple-element.6.a_ref, bf16[448,384]{1,0:T(8,128)(2,1)S(1)} %get-tuple-element.7.left_ref, bf16[384,896]{1,0:T(8,128)(2,1)S(1)} %get-tuple-element.8.right_ref, f32[1,64,448]{2,1,0:T(8,128)S(1)} %get-tuple-element.9.w_ref), custom_call_target="tpu_custom_call" | custom-call | tf_op jit(solution)/shard_map/tile_update/pallas_call | solution.py:268

commit v7 on v6

--- a/solution.py
+++ b/solution.py
@@ -264,7 +264,7 @@
         ),
         name="reflector_update",
     )(*(pltpu.with_memory_space_constraint(x, pltpu.HBM) for x in (reflectors.reshape(nc, h, n), matrix, factors[0])))
-    steps = 2
+    steps = 1
     return pl.pallas_call(
         update,
         grid=(steps,),

time: 30.2 us -> 30.2 us (level)
  no operation moved by 1% of the time
where the time goes in v7:
time: 30.2 us; the launch traced here: 30 us
  Pallas kernels  29.4 us (97%)
  between operations  0.64 us (2%)
    pallas_call x1, Pallas kernels, shards(): pl.pallas_call(functools.partial(kernel, nr, nc), out_shape=(jax.ShapeDty...  27.6 us
    pallas_call x1, Pallas kernels, shards(): pl.pallas_call(update, grid=(steps,), out_shape=(jax.ShapeDtypeStruct((m,...  1.76 us

profile of v7, /device:TPU:0, one launch (start us, length us, event | category | flops | bytes accessed | tf_op | source)
XLA Modules:
  0.0 30.0 jit_solution(8730204222331095878)
XLA Ops:
  0.6 27.6 %reflector_update.1 = (f32[448,896]{1,0:T(8,128)S(1)}, bf16[448,384]{1,0:T(8,128)(2,1)S(1)}, bf16[384,896]{1,0:T(8,128)(2,1)S(1)}, f32[1,64,448]{2,1,0:T(8,128)S(1)}) custom-call(f32[4,16,448]{2,1,0:T(8,128)} %bitcast.2, f32[448,896]{1,0:T(8,128)} %a_hbm.1, f32[64,64]{1,0:T(8,128)} %bitcast.3), custom_call_target="tpu_custom_call" | custom-call | tf_op jit(solution)/shard_map/reflector_update/pallas_call | solution.py:229
  28.3 1.8 %tile_update.1 = (f32[448,896]{1,0:T(8,128)}, f32[1,64,448]{2,1,0:T(8,128)}) custom-call(f32[448,896]{1,0:T(8,128)S(1)} %get-tuple-element.6.a_ref, bf16[448,384]{1,0:T(8,128)(2,1)S(1)} %get-tuple-element.7.left_ref, bf16[384,896]{1,0:T(8,128)(2,1)S(1)} %get-tuple-element.8.right_ref, f32[1,64,448]{2,1,0:T(8,128)S(1)} %get-tuple-element.9.w_ref), custom_call_target="tpu_custom_call" | custom-call | tf_op jit(solution)/shard_map/tile_update/pallas_call | solution.py:268
